TPU v7x, 32 devices: a whole 2x2x4 slice. The times are simulated.
32 devices in a mesh: blk: 4 (over x, core), grp: 8 (over z, y).
Axes of the slice: x: 2, y: 2, z: 4, core: 2. Of those that a mesh axis runs over, the one named last changes fastest.
Arguments:
- features: float32 [4, 8, 4, 64, 1024], P('blk', 'grp'), may hold values from -6 to 6
- inv_scale: float32 [64], replicated, may hold values from 0.01 to 0.2
- solution: float32 [4, 8, 4, 16, 1024], P('blk', 'grp'), may hold values from -6 to 6
- residual: float32 [4, 8, 4, 16, 1024], P('blk', 'grp'), may hold values from -6 to 6
- direction: float32 [4, 8, 4, 16, 1024], P('blk', 'grp'), may hold values from -6 to 6
- neighbours: int32 [4, 8, 4, 8], P('blk', 'grp'), may hold values from 0 to 127, as said below
Outputs:
- new_solution: float32 [4, 8, 4, 16, 1024], P('blk', 'grp')
- new_residual: float32 [4, 8, 4, 16, 1024], P('blk', 'grp')
- new_direction: float32 [4, 8, 4, 16, 1024], P('blk', 'grp')
Inputs may be any that keep to these rules, and one draw needn't show every extreme that they name: `neighbours`: each tile's list holds 8 different tile ids, among them the tile's own. The tile k of the device at blk b, grp g has id (b * 8 + g) * 4 + k. Listed tiles lie on the tile's own device, on the devices one step either way along blk (the blk index taken modulo 4), or on the devices one step either way along grp (no wrap).
All inputs are finite; a program needn't handle non-finite values.
Results may differ from a plain program's by a relative error of at most 0.00015.
Values sent between devices are 32-bit elements; how exact they have to be, the bound alone decides.
A program may use at most 64 MiB of HBM per device.

v0:
```python
import jax
import jax.numpy as jnp
from jax import lax
from jax.sharding import PartitionSpec as P

NOISE = 0.5


def extended(cells, sides, width, closed):
    for axis, dim in sides:
        count = lax.axis_size(axis)
        ends = count if closed else count - 1
        head = lax.slice_in_dim(cells, 0, width, axis=dim)
        tail = lax.slice_in_dim(cells, cells.shape[dim] - width, cells.shape[dim], axis=dim)
        cells = jnp.concatenate(
            [
                lax.ppermute(tail, axis, [(i, (i + 1) % count) for i in range(ends)]),
                cells,
                lax.ppermute(head, axis, [((i + 1) % count, i) for i in range(ends)]),
            ],
            axis=dim,
        )
    return cells


def wendland_terms(column_x, column_vec, row_x, row_norm):
    column_len = column_x.shape[1]
    stride = min(512, column_len)
    running = jnp.zeros((column_vec.shape[0], row_x.shape[1]), jnp.float32)
    for offset in range(0, column_len, stride):
        part_x = column_x[:, offset : offset + stride]
        part_norm = jnp.sum(part_x * part_x, axis=0)
        crossed = jnp.einsum(
            "fr,ft->rt",
            part_x,
            row_x,
            precision=lax.Precision.HIGHEST,
            preferred_element_type=jnp.float32,
        )
        squared = part_norm[:, None] + row_norm[None, :] - 2.0 * crossed
        radius = jnp.sqrt(jnp.maximum(squared, 0.0))
        remain = jnp.maximum(1.0 - radius, 0.0)
        weights = remain * remain * remain * remain * (4.0 * radius + 1.0)
        running = running + jnp.dot(
            column_vec[:, offset : offset + stride],
            weights,
            precision=lax.Precision.HIGHEST,
            preferred_element_type=jnp.float32,
        )
    return running


def per_device(features, inv_scale, solution, residual, direction, neighbours):
    tiles_here = features.shape[2]
    feat_count = features.shape[3]
    scaled = features * inv_scale[:, None]
    packed = jnp.concatenate([scaled, direction], axis=3)
    blk_count = lax.axis_size("blk")
    grp_count = lax.axis_size("grp")
    blk_index = lax.axis_index("blk")
    grp_index = lax.axis_index("grp")
    axes_all = (0, 1, 2, 4)
    start_norm = lax.psum(jnp.sum(residual * residual, axis=axes_all), ("blk", "grp"))
    looped = extended(packed, (("blk", 0),), 1, True)
    prior_blk = looped[0]
    next_blk = looped[2]
    sided = extended(packed, (("grp", 1),), 1, False)
    window = jnp.concatenate(
        [packed[0, 0], prior_blk[0], next_blk[0], sided[0, 0], sided[0, 2]], axis=0
    )
    tile_ids = neighbours[0, 0]
    device_ids = tile_ids // tiles_here
    within = tile_ids % tiles_here
    far_blk = device_ids // grp_count
    far_grp = device_ids % grp_count
    step_blk = (far_blk - blk_index + blk_count) % blk_count
    step_grp = far_grp - grp_index
    source = jnp.where(
        step_blk == 0,
        jnp.where(step_grp == 0, 0, jnp.where(step_grp < 0, 3, 4)),
        jnp.where(step_blk == 1, 2, 1),
    )
    local_ids = source * tiles_here + within

    def one_tile(inputs_row):
        row_x, slot_ids, row_dir = inputs_row
        row_norm = jnp.sum(row_x * row_x, axis=0)

        def accumulate(running, slot_id):
            column = lax.dynamic_index_in_dim(window, slot_id, 0, keepdims=False)
            return (
                running + wendland_terms(column[:feat_count], column[feat_count:], row_x, row_norm),
                None,
            )

        running, _ = lax.scan(accumulate, NOISE * row_dir, slot_ids)
        return running

    product = lax.map(one_tile, (scaled[0, 0], local_ids, direction[0, 0]))[None, None]
    curvature = lax.psum(jnp.sum(direction * product, axis=axes_all), ("blk", "grp"))
    step_size = start_norm / curvature
    new_residual = residual - step_size[:, None] * product
    fresh_norm = lax.psum(jnp.sum(new_residual * new_residual, axis=axes_all), ("blk", "grp"))
    new_solution = solution + step_size[:, None] * direction
    new_direction = new_residual + (fresh_norm / start_norm)[:, None] * direction
    return (new_solution, new_residual, new_direction)


def solution(mesh):
    in_specs = (
        P("blk", "grp", None, None, None),
        P(),
        P("blk", "grp", None, None, None),
        P("blk", "grp", None, None, None),
        P("blk", "grp", None, None, None),
        P("blk", "grp", None, None),
    )
    out_specs = (
        P("blk", "grp", None, None, None),
        P("blk", "grp", None, None, None),
        P("blk", "grp", None, None, None),
    )
    return jax.shard_map(
        per_device, mesh=mesh, in_specs=in_specs, out_specs=out_specs, check_vma=False
    )
```

profile of v0, /device:TPU:0, one launch (start us, length us, event | category | flops | bytes accessed | tf_op | source)
XLA Modules:
  0.0 574.3 jit_solution(15747647066727865135)
XLA Ops:
  5.7 5.3 collective-permute-start.2
  13.7 19.0 %collective-permute-done = f32[1,1,4,80,1024]{4,3,2,1,0:T(8,128)} collective-permute-done((f32[1,1,4,80,1024]{4,3,2,1,0:T(8,128)}, f32[1,1,4,80,1024]{4,3,2,1,0:T(8,128)}, u32[]{:S(2)}, u32[]{:S(2)}) %collective-permute-start) | collective-permute-done | bytes 1310752 | tf_op jit(solution)/shard_map/ppermute | solution.py:17
  36.6 29.8 %collective-permute-done.2 = f32[1,1,4,80,1024]{4,3,2,1,0:T(8,128)} collective-permute-done((f32[1,1,4,80,1024]{4,3,2,1,0:T(8,128)}, f32[1,1,4,80,1024]{4,3,2,1,0:T(8,128)}, u32[]{:S(2)}, u32[]{:S(2)}) %collective-permute-start.2) | collective-permute-done | bytes 1310752 | tf_op jit(solution)/shard_map/ppermute | solution.py:17
  69.3 2.7 copy-done
  72.0 419.8 %while.21 = (s32[]{:T(128)}, f32[4,16,1024]{2,1,0:T(8,128)S(1)}, f32[4,16,1024]{2,1,0:T(8,128)S(1)}, s32[4,8]{1,0:T(4,128)S(1)}, f32[4,64,1024]{2,1,0:T(8,128)},...) while((s32[]{:T(128)}, f32[4,16,1024]{2,1,0:T(8,128)S(1)}, ...), condition=%wide.region_8.9_spmd, body=%wide.region_2.8_spmd.sunk | while | flops 1019525120 | bytes 11227592 | solution.py:99
  73.1 103.9 %while.22 = (s32[]{:T(128)}, f32[16,1024]{1,0:T(8,128)S(1)}, s32[8]{0:T(128)S(1)}, f32[20,80,1024]{2,1,0:T(8,128)}, f32[1024]{0:T(1024)S(1)}, /*index=5*/f32[64,...) while((s32[]{:T(128)}, f32[16,1024]{1,0:T(8,128)S(1)}, s32[8]{0:T(128)S(1)}, ...), condition=%wide.region_7.7_spmd, body=%wide.region_4.6_spmd.sunk | while | flops 1019378688 | bytes 10436779 | solution.py:96
  83.6 2.4 fusion.94
  96.6 2.4 fusion.94
  161.6 2.4 fusion.94
  174.5 2.4 fusion.94
  178.0 103.9 %while.22 = (s32[]{:T(128)}, f32[16,1024]{1,0:T(8,128)S(1)}, s32[8]{0:T(128)S(1)}, f32[20,80,1024]{2,1,0:T(8,128)}, f32[1024]{0:T(1024)S(1)}, /*index=5*/f32[64,...) while((s32[]{:T(128)}, f32[16,1024]{1,0:T(8,128)S(1)}, s32[8]{0:T(128)S(1)}, ...), condition=%wide.region_7.7_spmd, body=%wide.region_4.6_spmd.sunk | while | flops 1019378688 | bytes 10436779 | solution.py:96
  188.6 2.4 fusion.94
  227.5 2.4 fusion.94
  279.5 2.4 fusion.94
  283.0 103.9 %while.22 = (s32[]{:T(128)}, f32[16,1024]{1,0:T(8,128)S(1)}, s32[8]{0:T(128)S(1)}, f32[20,80,1024]{2,1,0:T(8,128)}, f32[1024]{0:T(1024)S(1)}, /*index=5*/f32[64,...) while((s32[]{:T(128)}, f32[16,1024]{1,0:T(8,128)S(1)}, s32[8]{0:T(128)S(1)}, ...), condition=%wide.region_7.7_spmd, body=%wide.region_4.6_spmd.sunk | while | flops 1019378688 | bytes 10436779 | solution.py:96
  319.5 2.4 fusion.94
  332.5 2.4 fusion.94
  358.4 2.4 fusion.94
  387.9 103.9 %while.22 = (s32[]{:T(128)}, f32[16,1024]{1,0:T(8,128)S(1)}, s32[8]{0:T(128)S(1)}, f32[20,80,1024]{2,1,0:T(8,128)}, f32[1024]{0:T(1024)S(1)}, /*index=5*/f32[64,...) while((s32[]{:T(128)}, f32[16,1024]{1,0:T(8,128)S(1)}, s32[8]{0:T(128)S(1)}, ...), condition=%wide.region_7.7_spmd, body=%wide.region_4.6_spmd.sunk | while | flops 1019378688 | bytes 10436779 | solution.py:96
  424.4 2.4 fusion.94
  450.4 2.4 fusion.94
  463.3 2.4 fusion.94
  492.0 40.5 %all-reduce = (f32[16]{0:T(128)S(1)}, f32[16]{0:T(128)S(1)}) all-reduce(f32[16]{0:T(128)S(1)} %get-tuple-element.103, f32[16]{0:T(128)S(1)} %get-tuple-element.102), channel_id=1, replica_groups=mesh['blk'=4,'grp'=8] {'blk','grp'}, use_global_device_ids=true, to_apply=%region_1.0 | all-reduce | flops 32 | bytes 256 | tf_op jit(solution)/shard_map/psum | solution.py:63
  532.7 39.8 %psum.23 = f32[16]{0:T(128)S(1)} all-reduce(f32[16]{0:T(128)S(1)} %get-tuple-element.98), channel_id=1, replica_groups=mesh['blk'=4,'grp'=8] {'blk','grp'}, use_global_device_ids=true, to_apply=%region_12.13 | all-reduce | flops 16 | bytes 128 | tf_op jit(solution)/shard_map/psum | solution.py:103
  (292 shorter events, 341.0 us)
Async XLA Ops:
  0.6 1.5 copy-start.1
  0.6 11.7 %copy-start.6 = (s32[1,1,4,8]{3,2,1,0:T(4,128)S(1)}, s32[1,1,4,8]{3,2,1,0:T(4,128)}, u32[]{:S(2)}) copy-start(s32[1,1,4,8]{3,2,1,0:T(4,128)} %param.15) | copy-start | bytes 388
  2.1 10.4 %copy-start.2 = (f32[1,1,4,64,1024]{4,3,2,1,0:T(8,128)S(1)}, f32[1,1,4,64,1024]{4,3,2,1,0:T(8,128)}, u32[]{:S(2)}) copy-start(f32[1,1,4,64,1024]{4,3,2,1,0:T(8,128)} %param.10) | copy-start | bytes 3145732
  2.1 10.3 %copy-start.5 = (f32[64]{0:T(128)S(1)}, f32[64]{0:T(128)}, u32[]{:S(2)}) copy-start(f32[64]{0:T(128)} %param.11) | copy-start | bytes 772
  3.3 29.4 %collective-permute-start = (f32[1,1,4,80,1024]{4,3,2,1,0:T(8,128)}, f32[1,1,4,80,1024]{4,3,2,1,0:T(8,128)}, u32[]{:S(2)}, u32[]{:S(2)}) collective-permute-start(f32[1,1,4,80,1024]{4,3,2,1,0:T(8,128)} %pad_maximum_fusion), channel_id=1, source_target_pairs={{0,8},{8,16},{16,24},{24,0},{1,9},{9,17},{17,25},{25,1},{2,10},{10... | collective-permute-start | bytes 3932168 | tf_op jit(solution)/shard_map/ppermute | solution.py:17
  3.7 31.4 %collective-permute-start.1 = (f32[1,1,4,80,1024]{4,3,2,1,0:T(8,128)}, f32[1,1,4,80,1024]{4,3,2,1,0:T(8,128)}, u32[]{:S(2)}, u32[]{:S(2)}) collective-permute-start(f32[1,1,4,80,1024]{4,3,2,1,0:T(8,128)} %pad_maximum_fusion), channel_id=1, source_target_pairs={{8,0},{16,8},{24,16},{0,24},{9,1},{17,9},{25,17},{1,25},{10,2},{18... | collective-permute-start | bytes 3932168 | tf_op jit(solution)/shard_map/ppermute | solution.py:19
  5.7 60.7 %collective-permute-start.2 = (f32[1,1,4,80,1024]{4,3,2,1,0:T(8,128)}, f32[1,1,4,80,1024]{4,3,2,1,0:T(8,128)}, u32[]{:S(2)}, u32[]{:S(2)}) collective-permute-start(f32[1,1,4,80,1024]{4,3,2,1,0:T(8,128)} %pad_maximum_fusion), channel_id=1, source_target_pairs={{0,1},{1,2},{2,3},{3,4},{4,5},{5,6},{6,7},{8,9},{9,10},{10,11},{11... | collective-permute-start | bytes 3932168 | tf_op jit(solution)/shard_map/ppermute | solution.py:17
  11.0 56.8 %collective-permute-start.3 = (f32[1,1,4,80,1024]{4,3,2,1,0:T(8,128)}, f32[1,1,4,80,1024]{4,3,2,1,0:T(8,128)}, u32[]{:S(2)}, u32[]{:S(2)}) collective-permute-start(f32[1,1,4,80,1024]{4,3,2,1,0:T(8,128)} %pad_maximum_fusion), channel_id=1, source_target_pairs={{1,0},{2,1},{3,2},{4,3},{5,4},{6,5},{7,6},{9,8},{10,9},{11,10},{12... | collective-permute-start | bytes 3932168 | tf_op jit(solution)/shard_map/ppermute | solution.py:19
  69.3 2.7 copy-start
  72.0 419.8 %copy-start.3 = (f32[1,1,4,16,1024]{4,3,2,1,0:T(8,128)S(1)}, f32[1,1,4,16,1024]{4,3,2,1,0:T(8,128)}, u32[]{:S(2)}) copy-start(f32[1,1,4,16,1024]{4,3,2,1,0:T(8,128)} %param.13) | copy-start | bytes 786436
  532.7 41.6 %copy-start.4 = (f32[1,1,4,16,1024]{4,3,2,1,0:T(8,128)}, f32[1,1,4,16,1024]{4,3,2,1,0:T(8,128)S(1)}, u32[]{:S(2)}) copy-start(f32[1,1,4,16,1024]{4,3,2,1,0:T(8,128)S(1)} %get-tuple-element.99) | copy-start | bytes 786436
where the time goes:
time: 578 us; the launch traced here: 574 us
  matrix products  273 us (47%)
  local copies, waits for them, and re-layouts  85.9 us (15%)
  blocking collectives  80.2 us (14%)
  loops' own time  63.9 us (11%)
  waiting for transfers between devices  49.8 us (9%)
  other arithmetic  11.4 us (2%)
  starting transfers between devices  8.99 us (2%)
    dot_general x64, matrix products, wendland_terms(): jnp.dot(column_vec[:, offset:offset + stride], weights, precision=lax.Pre...  155 us
    dot_general x64, matrix products, wendland_terms(): jnp.einsum('fr,ft->rt', part_x, row_x, precision=lax.Precision.HIGHEST, p...  118 us
    another operation x4, loops' own time, one_tile(): running, _ = lax.scan(accumulate, NOISE * row_dir, slot_ids)  63.7 us
    ppermute x2, waiting for transfers between devices, extended(): lax.ppermute(tail, axis, [(i, (i + 1) % count) for i in range(ends)])  48.8 us
    psum x1, blocking collectives, per_device(): lax.psum(jnp.sum(residual * residual, axis=axes_all), ('blk', 'grp'))  40.5 us
    psum x1, blocking collectives, per_device(): lax.psum(jnp.sum(new_residual * new_residual, axis=axes_all), ('blk', 'gr...  39.8 us
    slice x32, local copies, waits for them, and re-layouts, accumulate(): column[:feat_count]  31.2 us
    slice x32, local copies, waits for them, and re-layouts, accumulate(): column[feat_count:]  27.3 us
  transfers between devices with their start and end apart: 4, of which 3 were waited for; matrix products, arithmetic and copies ran while one was open for 1% of the time, Pallas kernels for 0%

commit v1 on v0

v1 whole, which is shorter than its diff:
```python
import functools

import jax
import jax.numpy as jnp
from jax import lax
from jax.experimental import pallas as pl
from jax.experimental.pallas import tpu as pltpu
from jax.sharding import PartitionSpec as P

NOISE = 0.5
ROWS = 256
COLS = 256
LIMIT = 48 * 1024 * 1024
MESH = pl.DeviceIdType.MESH


def split_two(value):
    high = value.astype(jnp.bfloat16).astype(jnp.float32)
    return high, value - high


def split_norm(norm):
    first, rest = split_two(norm)
    second, third = split_two(rest)
    return [first, second, third]


def operand_rows(points, is_row):
    high, low = split_two(points)
    low = low.astype(jnp.bfloat16).astype(jnp.float32)
    feat = points.shape[0]
    kept = feat - 8
    norm = 16.0 * jnp.sum(high * (high + 2.0 * low), axis=0, keepdims=True)
    norm = norm + 16.0 * jnp.sum(low[:kept] * low[:kept], axis=0, keepdims=True)
    parts = split_norm(norm)
    shape = (8, points.shape[1])
    place = lax.broadcasted_iota(jnp.int32, shape, 0)
    first = 0 if is_row else 3
    tail = jnp.where(place < 6, 1.0, 0.0)
    for k in range(3):
        tail = jnp.where(place == first + k, jnp.broadcast_to(parts[k], shape), tail)
    if is_row:
        scaled_high, scaled_low = -32.0 * high, -32.0 * low
        return jnp.concatenate([scaled_high, scaled_high, scaled_low, scaled_low[:kept], tail], axis=0)
    return jnp.concatenate([high, low, high, low[:kept], tail], axis=0)


def vector_rows(vectors):
    high, low = split_two(vectors * (1.0 / 256.0))
    return jnp.concatenate([high, low], axis=0).astype(jnp.bfloat16)


def add_pair(row_ref, col_ref, vec_ref, acc_ref, s, t):
    tile = col_ref.shape[2]

    def one_block(step, _):
        rows = pl.ds(pl.multiple_of(step * ROWS, ROWS), ROWS)
        left = row_ref[s, rows, :]
        total = acc_ref[s, rows, :]
        for start in range(0, tile, COLS):
            squared = jnp.dot(left, col_ref[t, :, start : start + COLS], preferred_element_type=jnp.float32)
            squared = jnp.maximum(squared, 1e-30)
            radius = squared * lax.rsqrt(squared)
            remain = jnp.maximum(4.0 - radius, 0.0)
            square = remain * remain
            weight = (square * square) * (5.0 - remain)
            high = weight.astype(jnp.bfloat16)
            low = (weight - high.astype(jnp.float32)).astype(jnp.bfloat16)
            vec = vec_ref[t, :, start : start + COLS]
            dims = (((1,), (1,)), ((), ()))
            total = total + lax.dot_general(high, vec, dims, preferred_element_type=jnp.float32)
            total = total + lax.dot_general(low, vec, dims, preferred_element_type=jnp.float32)
        acc_ref[s, rows, :] = total
        return 0

    lax.fori_loop(0, tile // ROWS, one_block, 0)


def place_of(tile_id, tiles_here):
    blk_count, grp_count = lax.axis_size("blk"), lax.axis_size("grp")
    device = lax.div(tile_id, tiles_here)
    within = lax.rem(tile_id, tiles_here)
    step_blk = lax.rem(lax.div(device, grp_count) - lax.axis_index("blk") + blk_count, blk_count)
    step_grp = lax.rem(device, grp_count) - lax.axis_index("grp")
    return step_blk, step_grp, within


def walk(ids_ref, slot_of, row_ref, col_ref, vec_ref, acc_ref):
    tiles_here, listed = ids_ref.shape

    def visit(index, _):
        s = lax.div(index, listed)
        n = lax.rem(index, listed)
        slot = slot_of(*place_of(ids_ref[s, n], tiles_here))

        @pl.when(slot >= 0)
        def _():
            add_pair(row_ref, col_ref, vec_ref, acc_ref, s, slot)

        return 0

    lax.fori_loop(0, tiles_here * listed, visit, 0)


def folded(acc_ref, k, nvec):
    turned = acc_ref[k].T
    return turned[:nvec] + turned[nvec:]


def own_kernel(feat, ids_ref, packed_ref, row_ref, part_ref, col_ref, vec_ref, acc_ref):
    tiles = packed_ref.shape[0]
    nvec = packed_ref.shape[1] - feat
    for k in range(tiles):
        points = packed_ref[k, :feat]
        row_ref[k] = operand_rows(points, True).T.astype(jnp.bfloat16)
        col_ref[k] = operand_rows(points, False).astype(jnp.bfloat16)
        vec_ref[k] = vector_rows(packed_ref[k, feat:])
    acc_ref[...] = jnp.zeros_like(acc_ref)

    def slot_of(step_blk, step_grp, within):
        return jnp.where((step_blk == 0) & (step_grp == 0), within, -1)

    walk(ids_ref, slot_of, row_ref, col_ref, vec_ref, acc_ref)
    for k in range(tiles):
        part_ref[k] = NOISE * packed_ref[k, feat:] + folded(acc_ref, k, nvec)


def side_kernel(feat, along_blk, ids_ref, prior_ref, next_ref, row_ref, before_ref, part_ref, col_ref, vec_ref, acc_ref):
    tiles = prior_ref.shape[0]
    nvec = prior_ref.shape[1] - feat
    for source, ref in enumerate((prior_ref, next_ref)):
        for k in range(tiles):
            col_ref[source * tiles + k] = operand_rows(ref[k, :feat], False).astype(jnp.bfloat16)
            vec_ref[source * tiles + k] = vector_rows(ref[k, feat:])
    acc_ref[...] = jnp.zeros_like(acc_ref)

    def slot_of(step_blk, step_grp, within):
        if along_blk:
            return jnp.where(step_blk == 0, -1, jnp.where(step_blk == 1, tiles + within, within))
        side = jnp.where(step_grp < 0, within, tiles + within)
        return jnp.where((step_blk == 0) & (step_grp != 0), side, -1)

    walk(ids_ref, slot_of, row_ref, col_ref, vec_ref, acc_ref)
    for k in range(tiles):
        part_ref[k] = before_ref[k] + folded(acc_ref, k, nvec)


def scratch(cols, feat, nvec, tiles, tile):
    return [
        pltpu.VMEM((cols, 4 * feat, tile), jnp.bfloat16),
        pltpu.VMEM((cols, 2 * nvec, tile), jnp.bfloat16),
        pltpu.VMEM((tiles, tile, 2 * nvec), jnp.float32),
    ]


def cost(pairs, tile):
    return pl.CostEstimate(flops=int(pairs * tile * tile * 2048), bytes_accessed=4 << 20, transcendentals=0)


def in_smem():
    return pl.BlockSpec(memory_space=pltpu.SMEM)


def in_vmem():
    return pl.BlockSpec(memory_space=pltpu.VMEM)


def own_pairs(ids, packed, feat):
    tiles, width, tile = packed.shape
    nvec = width - feat
    return pl.pallas_call(
        functools.partial(own_kernel, feat),
        out_shape=(
            jax.ShapeDtypeStruct((tiles, tile, 4 * feat), jnp.bfloat16),
            jax.ShapeDtypeStruct((tiles, nvec, tile), jnp.float32),
        ),
        in_specs=[in_smem(), in_vmem()],
        out_specs=(in_vmem(), in_vmem()),
        scratch_shapes=scratch(tiles, feat, nvec, tiles, tile),
        compiler_params=pltpu.CompilerParams(vmem_limit_bytes=LIMIT),
        cost_estimate=cost(8, tile),
        name="own_pairs",
    )(ids, packed)


def side_pairs(ids, prior, following, rows, before, feat, along_blk):
    tiles, width, tile = prior.shape
    nvec = width - feat
    return pl.pallas_call(
        functools.partial(side_kernel, feat, along_blk),
        out_shape=jax.ShapeDtypeStruct((tiles, nvec, tile), jnp.float32),
        in_specs=[in_smem()] + [in_vmem()] * 4,
        out_specs=in_vmem(),
        scratch_shapes=scratch(2 * tiles, feat, nvec, tiles, tile),
        compiler_params=pltpu.CompilerParams(vmem_limit_bytes=LIMIT),
        cost_estimate=cost(12, tile),
        name="blk_pairs" if along_blk else "grp_pairs",
    )(ids, prior, following, rows, before)


def sums_kernel(part_ref, residual_ref, direction_ref, out_ref, held_ref, blk_ref, grp_ref, send_sem, blk_sem, grp_sem):
    blk_count, grp_count = lax.axis_size("blk"), lax.axis_size("grp")
    blk_index, grp_index = lax.axis_index("blk"), lax.axis_index("grp")
    barrier = pltpu.get_barrier_semaphore()

    def blk_partner(k):
        return (lax.rem(blk_index + k, blk_count), grp_index)

    def grp_partner(k):
        return (blk_index, lax.rem(grp_index + k, grp_count))

    def greet(partner, k, _):
        pl.semaphore_signal(barrier, inc=1, device_id=partner(k), device_id_type=MESH)
        return 0

    lax.fori_loop(1, blk_count, functools.partial(greet, blk_partner), 0)
    lax.fori_loop(1, grp_count, functools.partial(greet, grp_partner), 0)

    nvec = part_ref.shape[1]
    lane = lax.broadcasted_iota(jnp.int32, (nvec, 128), 1)

    def total_of(first_ref, second_ref):
        both = jnp.sum(first_ref[...] * second_ref[...], axis=0)
        return jnp.sum(both, axis=1, keepdims=True)

    held = jnp.zeros((nvec, 128), jnp.float32)
    pairs = (
        (residual_ref, residual_ref),
        (direction_ref, part_ref),
        (residual_ref, part_ref),
        (part_ref, part_ref),
    )
    for k, (first_ref, second_ref) in enumerate(pairs):
        held = jnp.where(lane == k, total_of(first_ref, second_ref), held)
    held_ref[0] = held
    pl.semaphore_wait(barrier, blk_count + grp_count - 2)

    def swap(source, landing, sems, partner, count):
        def copy_of(k):
            return pltpu.make_async_remote_copy(
                src_ref=source,
                dst_ref=landing.at[k],
                send_sem=send_sem.at[k],
                recv_sem=sems.at[k],
                device_id=partner(k),
                device_id_type=MESH,
            )

        def begin(k, _):
            copy_of(k).start()
            return 0

        def end(k, _):
            copy_of(k).wait()
            return 0

        lax.fori_loop(1, count, begin, 0)
        lax.fori_loop(1, count, end, 0)

        def add(k, total):
            return total + landing[k]

        return lax.fori_loop(1, count, add, source[...])

    held_ref[1] = swap(held_ref.at[0], blk_ref, blk_sem, blk_partner, blk_count)
    out_ref[...] = swap(held_ref.at[1], grp_ref, grp_sem, grp_partner, grp_count)


def summed(part, residual, direction):
    nvec = part.shape[1]
    blk_count, grp_count = lax.axis_size("blk"), lax.axis_size("grp")
    return pl.pallas_call(
        sums_kernel,
        out_shape=jax.ShapeDtypeStruct((nvec, 128), jnp.float32),
        in_specs=[in_vmem()] * 3,
        out_specs=in_vmem(),
        scratch_shapes=[
            pltpu.VMEM((2, nvec, 128), jnp.float32),
            pltpu.VMEM((blk_count, nvec, 128), jnp.float32),
            pltpu.VMEM((grp_count, nvec, 128), jnp.float32),
            pltpu.SemaphoreType.DMA((max(blk_count, grp_count),)),
            pltpu.SemaphoreType.DMA((blk_count,)),
            pltpu.SemaphoreType.DMA((grp_count,)),
        ],
        compiler_params=pltpu.CompilerParams(collective_id=0, has_side_effects=True),
        name="sums",
    )(part, residual, direction)


def per_device(features, inv_scale, solution, residual, direction, neighbours):
    feat = features.shape[3]
    blk_count, grp_count = lax.axis_size("blk"), lax.axis_size("grp")
    packed = jnp.concatenate([features[0, 0] * inv_scale[:, None], direction[0, 0]], axis=1)
    ids = neighbours[0, 0]
    up = [(i, (i + 1) % blk_count) for i in range(blk_count)]
    down = [((i + 1) % blk_count, i) for i in range(blk_count)]
    prior_blk = lax.ppermute(packed, "blk", up)
    next_blk = lax.ppermute(packed, "blk", down)
    prior_grp = lax.ppermute(packed, "grp", [(i, i + 1) for i in range(grp_count - 1)])
    next_grp = lax.ppermute(packed, "grp", [(i + 1, i) for i in range(grp_count - 1)])
    rows, part = own_pairs(ids, packed, feat)
    part = side_pairs(ids, prior_blk, next_blk, rows, part, feat, True)
    part = side_pairs(ids, prior_grp, next_grp, rows, part, feat, False)
    sums = summed(part, residual[0, 0], direction[0, 0])
    start_norm, curvature, crossed, length = (sums[:, k : k + 1] for k in range(4))
    step = start_norm / curvature
    fresh_norm = jnp.maximum(start_norm + step * (step * length - 2.0 * crossed), 0.0)
    new_residual = residual - step * part
    new_solution = solution + step * direction
    new_direction = new_residual + (fresh_norm / start_norm) * direction
    return (new_solution, new_residual, new_direction)


def solution(mesh):
    split = P("blk", "grp", None, None, None)
    in_specs = (split, P(), split, split, split, P("blk", "grp", None, None))
    return jax.shard_map(per_device, mesh=mesh, in_specs=in_specs, out_specs=(split, split, split), check_vma=False)
```

time: 578 us -> 167 us (0.29)
  matrix products: 273 us -> 0 us
  Pallas kernels: 0 us -> 153 us
  local copies, waits for them, and re-layouts: 85.9 us -> 0.74 us
  blocking collectives: 80.2 us -> 0 us
  loops' own time: 63.9 us -> 0 us
  waiting for transfers between devices: 49.8 us -> 0.02 us
  other arithmetic: 11.4 us -> 4.59 us
    dot_general x128 -> x0, matrix products: 273 us -> none  [the longest x64 155 us: wendland_terms(): jnp.dot(column_vec[:, offset:offset + stride], weights, precision=lax.Pre...]
    pallas_call x0 -> x4, Pallas kernels: none -> 153 us  [the longest x2 95.4 us: side_pairs(): pl.pallas_call(functools.partial(side_kernel, feat, along_blk), out_shape...]
    psum x2 -> x0, blocking collectives: 80.2 us -> none  [the longest x1 40.5 us: per_device(): lax.psum(jnp.sum(residual * residual, axis=axes_all), ('blk', 'grp'))]
    another operation x5 -> x0, loops' own time: 63.9 us -> none  [the longest x4 63.7 us: one_tile(): running, _ = lax.scan(accumulate, NOISE * row_dir, slot_ids)]
    slice x64 -> x0, local copies, waits for them, and re-layouts: 58.5 us -> none  [the longest x32 31.2 us: accumulate(): column[:feat_count]]
    ppermute x4, waiting for transfers between devices: 49.8 us -> 0.02 us  [the longest x1 0.01 us: per_device(): prior_blk = lax.ppermute(packed, 'blk', up)]
    dynamic_slice x32 -> x0, local copies, waits for them, and re-layouts: 18.8 us -> none  [one_tile(): running, _ = lax.scan(accumulate, NOISE * row_dir, slot_ids)]
    unnamed x17 -> x12, local copies, waits for them, and re-layouts: 7.1 us -> 0.74 us
  transfers between devices with their start and end apart: 4 -> 4, of which waited for: 3 -> 0; matrix products, arithmetic and copies ran while one was open for 1% -> 0% of each run, Pallas kernels for 0% -> 67%
where the time goes in v1:
time: 167 us
  Pallas kernels  153 us (92%)
  starting transfers between devices  8.03 us (5%)
  other arithmetic  4.59 us (3%)
    pallas_call x2, Pallas kernels, side_pairs(): pl.pallas_call(functools.partial(side_kernel, feat, along_blk), out_shape...  95.4 us
    pallas_call x1, Pallas kernels, own_pairs(): pl.pallas_call(functools.partial(own_kernel, feat), out_shape=(jax.ShapeD...  43.5 us
    pallas_call x1, Pallas kernels, summed(): pl.pallas_call(sums_kernel, out_shape=jax.ShapeDtypeStruct((nvec, 128), j...  14.1 us
    ppermute x1, starting transfers between devices, per_device(): lax.ppermute(packed, 'grp', [(i, i + 1) for i in range(grp_count - 1)])  4.25 us
  transfers between devices with their start and end apart: 4, of which 0 were waited for; matrix products, arithmetic and copies ran while one was open for 0% of the time, Pallas kernels for 67%

profile of v1, /device:TPU:0, one launch (start us, length us, event | category | flops | bytes accessed | tf_op | source)
XLA Modules:
  0.0 167.2 jit_solution(12021073622818199562)
XLA Ops:
  0.6 0.0 copy-start.2
  0.6 1.4 bitcast_multiply_fusion
  2.1 0.0 copy-done.2
  2.1 0.0 copy-start.1
  2.1 0.1 pad_maximum_fusion.packed_ref
  2.3 0.5 collective-permute-start.2
  2.8 2.0 %collective-permute-start.3 = (f32[4,80,1024]{2,1,0:T(8,128)S(1)}, f32[4,80,1024]{2,1,0:T(8,128)S(1)}, u32[]{:S(2)}, u32[]{:S(2)}) collective-permute-start(f32[4,80,1024]{2,1,0:T(8,128)S(1)} %pad_maximum_fusion.packed_ref), channel_id=1, source_target_pairs={{8,0},{16,8},{24,16},{0,24},{9,1},{17,9},{25,17},{1,25},{10,2},{18... | collective-permute-start | bytes 3932168 | tf_op jit(solution)/shard_map/ppermute | solution.py:298
  4.7 4.2 %collective-permute-start = (f32[4,80,1024]{2,1,0:T(8,128)S(1)}, f32[4,80,1024]{2,1,0:T(8,128)S(1)}, u32[]{:S(2)}, u32[]{:S(2)}) collective-permute-start(f32[4,80,1024]{2,1,0:T(8,128)S(1)} %pad_maximum_fusion.packed_ref), channel_id=1, source_target_pairs={{0,1},{1,2},{2,3},{3,4},{4,5},{5,6},{6,7},{8,9},{9,10},{10,11},{11... | collective-permute-start | bytes 3932168 | tf_op jit(solution)/shard_map/ppermute | solution.py:299
  9.0 1.3 collective-permute-start.1
  10.3 43.5 %own_pairs.1 = (bf16[4,1024,256]{2,1,0:T(8,128)(2,1)S(1)}, f32[4,16,1024]{2,1,0:T(8,128)S(1)}) custom-call(s32[4,8]{1,0:T(4,128)S(1)} %bitcast.8, f32[4,80,1024]{2,1,0:T(8,128)S(1)} %pad_maximum_fusion.packed_ref), custom_call_target="tpu_custom_call" | custom-call | flops 17179869184 | bytes 4194304 | tf_op jit(solution)/shard_map/own_pairs/pallas_call | solution.py:171
  53.8 0.0 collective-permute-done.2.prior_ref
  53.9 0.0 collective-permute-done.3.next_ref
  53.9 67.9 %blk_pairs.1.before_ref = f32[4,16,1024]{2,1,0:T(8,128)S(1)} custom-call(s32[4,8]{1,0:T(4,128)S(1)} %bitcast.9, f32[4,80,1024]{2,1,0:T(8,128)S(1)} %collective-permute-done.2.prior_ref, f32[4,80,1024]{2,1,0:T(8,128)S(1)} %collective-permute-done.3.next_ref, bf16[4,1024,256]{2,1,0:T(8,128)(2,1)S(1)} %get-tuple-element.5.row_ref, ...), custom_call_target="tpu_custom_call" | custom-call | flops 25769803776 | bytes 4194304 | tf_op jit(solution)/shard_map/blk_pairs/pallas_call | solution.py:189
  121.7 0.0 copy-start.3
  121.7 0.0 copy-start.4
  121.8 0.0 copy-start.5
  121.8 0.0 collective-permute-done.prior_ref
  121.8 0.0 collective-permute-done.1.next_ref
  121.8 27.5 %grp_pairs.1.part_ref = f32[4,16,1024]{2,1,0:T(8,128)S(1)} custom-call(s32[4,8]{1,0:T(4,128)S(1)} %bitcast.10, f32[4,80,1024]{2,1,0:T(8,128)S(1)} %collective-permute-done.prior_ref, f32[4,80,1024]{2,1,0:T(8,128)S(1)} %collective-permute-done.1.next_ref, bf16[4,1024,256]{2,1,0:T(8,128)(2,1)S(1)} %get-tuple-element.5.row_ref, ...), custom_call_target="tpu_custom_call" | custom-call | flops 25769803776 | bytes 4194304 | tf_op jit(solution)/shard_map/grp_pairs/pallas_call | solution.py:189
  149.3 0.0 copy-start
  149.3 0.7 copy-done
  150.0 14.1 %sums.1 = f32[16,128]{1,0:T(8,128)} custom-call(f32[4,16,1024]{2,1,0:T(8,128)} %copy-done, f32[4,16,1024]{2,1,0:T(8,128)} %bitcast.13, f32[4,16,1024]{2,1,0:T(8,128)} %bitcast.11), custom_call_target="tpu_custom_call" | custom-call | tf_op jit(solution)/shard_map/sums/pallas_call | solution.py:272
  164.2 1.0 fusion
  165.2 2.0 %multiply_add_fusion = (f32[1,1,4,16,1024]{4,3,2,1,0:T(8,128)}, f32[1,1,4,16,1024]{4,3,2,1,0:T(8,128)}, f32[1,1,4,16,1024]{4,3,2,1,0:T(8,128)}) fusion(f32[1,1,4,16,1024]{4,3,2,1,0:T(8,128)S(1)} %copy-done.3, f32[16]{0:T(128)S(1)} %get-tuple-element.7, f32[1,1,4,16,1024]{4,3,2,1,0:T(8,128)S(1)} %copy-done.4, f32[4,16,1024]{2,1,0:T(8,128)} %copy-done, ...), kind=kLoop, calls=%fused_computation.3 | loop fusion | flops 393216 | bytes 1835136 | tf_op jit(solution)/shard_map/add | solution.py:310
  (4 shorter events, 0.0 us)
Async XLA Ops:
  0.6 1.5 copy-start.2
  2.1 8.2 %copy-start.1 = (s32[1,1,4,8]{3,2,1,0:T(4,128)S(1)}, s32[1,1,4,8]{3,2,1,0:T(4,128)}, u32[]{:S(2)}) copy-start(s32[1,1,4,8]{3,2,1,0:T(4,128)} %param.11) | copy-start | bytes 388
  2.3 51.6 %collective-permute-start.2 = (f32[4,80,1024]{2,1,0:T(8,128)S(1)}, f32[4,80,1024]{2,1,0:T(8,128)S(1)}, u32[]{:S(2)}, u32[]{:S(2)}) collective-permute-start(f32[4,80,1024]{2,1,0:T(8,128)S(1)} %pad_maximum_fusion.packed_ref), channel_id=1, source_target_pairs={{0,8},{8,16},{16,24},{24,0},{1,9},{9,17},{17,25},{25,1},{2,10},{10... | collective-permute-start | bytes 3932168 | tf_op jit(solution)/shard_map/ppermute | solution.py:297
  2.8 51.1 %collective-permute-start.3 = (f32[4,80,1024]{2,1,0:T(8,128)S(1)}, f32[4,80,1024]{2,1,0:T(8,128)S(1)}, u32[]{:S(2)}, u32[]{:S(2)}) collective-permute-start(f32[4,80,1024]{2,1,0:T(8,128)S(1)} %pad_maximum_fusion.packed_ref), channel_id=1, source_target_pairs={{8,0},{16,8},{24,16},{0,24},{9,1},{17,9},{25,17},{1,25},{10,2},{18... | collective-permute-start | bytes 3932168 | tf_op jit(solution)/shard_map/ppermute | solution.py:298
  4.7 117.0 %collective-permute-start = (f32[4,80,1024]{2,1,0:T(8,128)S(1)}, f32[4,80,1024]{2,1,0:T(8,128)S(1)}, u32[]{:S(2)}, u32[]{:S(2)}) collective-permute-start(f32[4,80,1024]{2,1,0:T(8,128)S(1)} %pad_maximum_fusion.packed_ref), channel_id=1, source_target_pairs={{0,1},{1,2},{2,3},{3,4},{4,5},{5,6},{6,7},{8,9},{9,10},{10,11},{11... | collective-permute-start | bytes 3932168 | tf_op jit(solution)/shard_map/ppermute | solution.py:299
  9.0 112.8 %collective-permute-start.1 = (f32[4,80,1024]{2,1,0:T(8,128)S(1)}, f32[4,80,1024]{2,1,0:T(8,128)S(1)}, u32[]{:S(2)}, u32[]{:S(2)}) collective-permute-start(f32[4,80,1024]{2,1,0:T(8,128)S(1)} %pad_maximum_fusion.packed_ref), channel_id=1, source_target_pairs={{1,0},{2,1},{3,2},{4,3},{5,4},{6,5},{7,6},{9,8},{10,9},{11,10},{12... | collective-permute-start | bytes 3932168 | tf_op jit(solution)/shard_map/ppermute | solution.py:300
  121.7 43.5 %copy-start.3 = (f32[1,1,4,16,1024]{4,3,2,1,0:T(8,128)S(1)}, f32[1,1,4,16,1024]{4,3,2,1,0:T(8,128)}, u32[]{:S(2)}) copy-start(f32[1,1,4,16,1024]{4,3,2,1,0:T(8,128)} %param.10) | copy-start | bytes 786436
  121.7 43.5 %copy-start.4 = (f32[1,1,4,16,1024]{4,3,2,1,0:T(8,128)S(1)}, f32[1,1,4,16,1024]{4,3,2,1,0:T(8,128)}, u32[]{:S(2)}) copy-start(f32[1,1,4,16,1024]{4,3,2,1,0:T(8,128)} %param.9) | copy-start | bytes 786436
  121.8 43.5 %copy-start.5 = (f32[1,1,4,16,1024]{4,3,2,1,0:T(8,128)S(1)}, f32[1,1,4,16,1024]{4,3,2,1,0:T(8,128)}, u32[]{:S(2)}) copy-start(f32[1,1,4,16,1024]{4,3,2,1,0:T(8,128)} %param.8) | copy-start | bytes 786436
  149.3 0.7 copy-start

commit v2 on v1

--- a/solution.py
+++ b/solution.py
@@ -8,7 +8,7 @@
 from jax.sharding import PartitionSpec as P
 
 NOISE = 0.5
-ROWS = 256
+ROWS = 512
 COLS = 256
 LIMIT = 48 * 1024 * 1024
 MESH = pl.DeviceIdType.MESH
@@ -51,29 +51,30 @@
 
 
 def add_pair(row_ref, col_ref, vec_ref, acc_ref, s, t):
-    tile = col_ref.shape[2]
-
-    def one_block(step, _):
-        rows = pl.ds(pl.multiple_of(step * ROWS, ROWS), ROWS)
-        left = row_ref[s, rows, :]
-        total = acc_ref[s, rows, :]
-        for start in range(0, tile, COLS):
-            squared = jnp.dot(left, col_ref[t, :, start : start + COLS], preferred_element_type=jnp.float32)
-            squared = jnp.maximum(squared, 1e-30)
-            radius = squared * lax.rsqrt(squared)
-            remain = jnp.maximum(4.0 - radius, 0.0)
-            square = remain * remain
-            weight = (square * square) * (5.0 - remain)
-            high = weight.astype(jnp.bfloat16)
-            low = (weight - high.astype(jnp.float32)).astype(jnp.bfloat16)
-            vec = vec_ref[t, :, start : start + COLS]
-            dims = (((1,), (1,)), ((), ()))
-            total = total + lax.dot_general(high, vec, dims, preferred_element_type=jnp.float32)
-            total = total + lax.dot_general(low, vec, dims, preferred_element_type=jnp.float32)
-        acc_ref[s, rows, :] = total
-        return 0
-
-    lax.fori_loop(0, tile // ROWS, one_block, 0)
+    depth, tile = row_ref.shape[1:]
+    places = [(r, c) for c in range(0, tile, COLS) for r in range(0, tile, ROWS)]
+
+    def squared_of(place):
+        r, c = place
+        return jnp.dot(col_ref[t, r : r + ROWS, :], row_ref[s, :, c : c + COLS], preferred_element_type=jnp.float32)
+
+    ahead = squared_of(places[0])
+    for k, (r, c) in enumerate(places):
+        squared = jnp.maximum(ahead, 1e-30)
+        if k + 1 < len(places):
+            ahead = squared_of(places[k + 1])
+        radius = squared * lax.rsqrt(squared)
+        remain = jnp.maximum(4.0 - radius, 0.0)
+        square = remain * remain
+        weight = (square * square) * (5.0 - remain)
+        high = weight.astype(jnp.bfloat16)
+        low = (weight - high.astype(jnp.float32)).astype(jnp.bfloat16)
+        vec = vec_ref[t, :, r : r + ROWS]
+        acc_ref[s, :, c : c + COLS] += jnp.dot(
+            jnp.concatenate([vec, vec], axis=1),
+            jnp.concatenate([high, low], axis=0),
+            preferred_element_type=jnp.float32,
+        )
 
 
 def place_of(tile_id, tiles_here):
@@ -103,8 +104,7 @@
 
 
 def folded(acc_ref, k, nvec):
-    turned = acc_ref[k].T
-    return turned[:nvec] + turned[nvec:]
+    return acc_ref[k, :nvec] + acc_ref[k, nvec:]
 
 
 def own_kernel(feat, ids_ref, packed_ref, row_ref, part_ref, col_ref, vec_ref, acc_ref):
@@ -112,8 +112,8 @@
     nvec = packed_ref.shape[1] - feat
     for k in range(tiles):
         points = packed_ref[k, :feat]
-        row_ref[k] = operand_rows(points, True).T.astype(jnp.bfloat16)
-        col_ref[k] = operand_rows(points, False).astype(jnp.bfloat16)
+        row_ref[k] = operand_rows(points, True).astype(jnp.bfloat16)
+        col_ref[k] = operand_rows(points, False).astype(jnp.bfloat16).T
         vec_ref[k] = vector_rows(packed_ref[k, feat:])
     acc_ref[...] = jnp.zeros_like(acc_ref)
 
@@ -130,7 +130,7 @@
     nvec = prior_ref.shape[1] - feat
     for source, ref in enumerate((prior_ref, next_ref)):
         for k in range(tiles):
-            col_ref[source * tiles + k] = operand_rows(ref[k, :feat], False).astype(jnp.bfloat16)
+            col_ref[source * tiles + k] = operand_rows(ref[k, :feat], False).astype(jnp.bfloat16).T
             vec_ref[source * tiles + k] = vector_rows(ref[k, feat:])
     acc_ref[...] = jnp.zeros_like(acc_ref)
 
@@ -147,9 +147,9 @@
 
 def scratch(cols, feat, nvec, tiles, tile):
     return [
-        pltpu.VMEM((cols, 4 * feat, tile), jnp.bfloat16),
+        pltpu.VMEM((cols, tile, 4 * feat), jnp.bfloat16),
         pltpu.VMEM((cols, 2 * nvec, tile), jnp.bfloat16),
-        pltpu.VMEM((tiles, tile, 2 * nvec), jnp.float32),
+        pltpu.VMEM((tiles, 2 * nvec, tile), jnp.float32),
     ]
 
 
@@ -171,7 +171,7 @@
     return pl.pallas_call(
         functools.partial(own_kernel, feat),
         out_shape=(
-            jax.ShapeDtypeStruct((tiles, tile, 4 * feat), jnp.bfloat16),
+            jax.ShapeDtypeStruct((tiles, 4 * feat, tile), jnp.bfloat16),
             jax.ShapeDtypeStruct((tiles, nvec, tile), jnp.float32),
         ),
         in_specs=[in_smem(), in_vmem()],
@@ -263,7 +263,11 @@
         return lax.fori_loop(1, count, add, source[...])
 
     held_ref[1] = swap(held_ref.at[0], blk_ref, blk_sem, blk_partner, blk_count)
-    out_ref[...] = swap(held_ref.at[1], grp_ref, grp_sem, grp_partner, grp_count)
+    sums = swap(held_ref.at[1], grp_ref, grp_sem, grp_partner, grp_count)
+    start_norm, curvature, crossed, length = (sums[:, k : k + 1] for k in range(4))
+    step = start_norm / curvature
+    fresh_norm = jnp.maximum(start_norm + step * (step * length - 2.0 * crossed), 0.0)
+    out_ref[...] = jnp.where(lane == 0, step, fresh_norm / start_norm)
 
 
 def summed(part, residual, direction):
@@ -301,13 +305,11 @@
     rows, part = own_pairs(ids, packed, feat)
     part = side_pairs(ids, prior_blk, next_blk, rows, part, feat, True)
     part = side_pairs(ids, prior_grp, next_grp, rows, part, feat, False)
-    sums = summed(part, residual[0, 0], direction[0, 0])
-    start_norm, curvature, crossed, length = (sums[:, k : k + 1] for k in range(4))
-    step = start_norm / curvature
-    fresh_norm = jnp.maximum(start_norm + step * (step * length - 2.0 * crossed), 0.0)
+    factors = summed(part, residual[0, 0], direction[0, 0])
+    step, ratio = factors[:, :1], factors[:, 1:2]
     new_residual = residual - step * part
     new_solution = solution + step * direction
-    new_direction = new_residual + (fresh_norm / start_norm) * direction
+    new_direction = new_residual + ratio * direction
     return (new_solution, new_residual, new_direction)
 
 

time: 167 us -> 120 us (0.72)
  Pallas kernels: 153 us -> 102 us
  waiting for transfers between devices: 0.02 us -> 4.33 us
    pallas_call x2, Pallas kernels: 95.4 us -> 56.9 us  [side_pairs(): pl.pallas_call(functools.partial(side_kernel, feat, along_blk), out_shape...]
    pallas_call x1, Pallas kernels: 43.5 us -> 19.2 us  [own_pairs(): pl.pallas_call(functools.partial(own_kernel, feat), out_shape=(jax.ShapeD...]
    pallas_call x1, Pallas kernels: 14.1 us -> 25.9 us  [summed(): pl.pallas_call(sums_kernel, out_shape=jax.ShapeDtypeStruct((nvec, 128), j...]
    ppermute x1, waiting for transfers between devices: 0.01 us -> 2.49 us  [per_device(): next_blk = lax.ppermute(packed, 'blk', down)]
    ppermute x1, waiting for transfers between devices: 0.01 us -> 1.84 us  [per_device(): prior_blk = lax.ppermute(packed, 'blk', up)]
  transfers between devices with their start and end apart: 4 -> 4, of which waited for: 0 -> 2; matrix products, arithmetic and copies ran while one was open for 0% -> 0% of each run, Pallas kernels for 67% -> 50%
where the time goes in v2:
time: 120 us
  Pallas kernels  102 us (85%)
  starting transfers between devices  8.03 us (7%)
  waiting for transfers between devices  4.33 us (4%)
  other arithmetic  3.55 us (3%)
  local copies, waits for them, and re-layouts  1.68 us (1%)
    pallas_call x2, Pallas kernels, side_pairs(): pl.pallas_call(functools.partial(side_kernel, feat, along_blk), out_shape...  56.9 us
    pallas_call x1, Pallas kernels, summed(): pl.pallas_call(sums_kernel, out_shape=jax.ShapeDtypeStruct((nvec, 128), j...  25.9 us
    pallas_call x1, Pallas kernels, own_pairs(): pl.pallas_call(functools.partial(own_kernel, feat), out_shape=(jax.ShapeD...  19.2 us
    ppermute x1, starting transfers between devices, per_device(): lax.ppermute(packed, 'grp', [(i, i + 1) for i in range(grp_count - 1)])  4.25 us
    ppermute x1, waiting for transfers between devices, per_device(): next_blk = lax.ppermute(packed, 'blk', down)  2.49 us
  transfers between devices with their start and end apart: 4, of which 2 were waited for; matrix products, arithmetic and copies ran while one was open for 0% of the time, Pallas kernels for 50%

profile of v2, /device:TPU:0, one launch (start us, length us, event | category | flops | bytes accessed | tf_op | source)
XLA Modules:
  0.0 120.4 jit_solution(14356578388577196908)
XLA Ops:
  0.6 0.0 copy-start.2
  0.6 1.4 %bitcast_multiply_fusion = f32[4,64,1024]{2,1,0:T(8,128)S(1)} fusion(f32[1,1,4,64,1024]{4,3,2,1,0:T(8,128)} %param.6, f32[64]{0:T(128)} %param.7), kind=kLoop, calls=%fused_computation.1 | loop fusion | flops 262144 | bytes 2097408 | tf_op jit(solution)/shard_map/mul | solution.py:297
  2.1 0.0 copy-start.1
  2.1 0.1 pad_maximum_fusion.packed_ref
  2.3 0.5 collective-permute-start.2
  2.8 2.0 %collective-permute-start.3 = (f32[4,80,1024]{2,1,0:T(8,128)S(1)}, f32[4,80,1024]{2,1,0:T(8,128)S(1)}, u32[]{:S(2)}, u32[]{:S(2)}) collective-permute-start(f32[4,80,1024]{2,1,0:T(8,128)S(1)} %pad_maximum_fusion.packed_ref), channel_id=1, source_target_pairs={{8,0},{16,8},{24,16},{0,24},{9,1},{17,9},{25,17},{1,25},{10,2},{18... | collective-permute-start | bytes 3932168 | tf_op jit(solution)/shard_map/ppermute | solution.py:302
  4.7 4.2 %collective-permute-start = (f32[4,80,1024]{2,1,0:T(8,128)S(1)}, f32[4,80,1024]{2,1,0:T(8,128)S(1)}, u32[]{:S(2)}, u32[]{:S(2)}) collective-permute-start(f32[4,80,1024]{2,1,0:T(8,128)S(1)} %pad_maximum_fusion.packed_ref), channel_id=1, source_target_pairs={{0,1},{1,2},{2,3},{3,4},{4,5},{5,6},{6,7},{8,9},{9,10},{10,11},{11... | collective-permute-start | bytes 3932168 | tf_op jit(solution)/shard_map/ppermute | solution.py:303
  9.0 1.3 %collective-permute-start.1 = (f32[4,80,1024]{2,1,0:T(8,128)S(1)}, f32[4,80,1024]{2,1,0:T(8,128)S(1)}, u32[]{:S(2)}, u32[]{:S(2)}) collective-permute-start(f32[4,80,1024]{2,1,0:T(8,128)S(1)} %pad_maximum_fusion.packed_ref), channel_id=1, source_target_pairs={{1,0},{2,1},{3,2},{4,3},{5,4},{6,5},{7,6},{9,8},{10,9},{11,10},{12... | collective-permute-start | bytes 3932168 | tf_op jit(solution)/shard_map/ppermute | solution.py:304
  10.3 19.2 %own_pairs.1 = (bf16[4,256,1024]{2,1,0:T(8,128)(2,1)S(1)}, f32[4,16,1024]{2,1,0:T(8,128)S(1)}) custom-call(s32[4,8]{1,0:T(4,128)S(1)} %bitcast.8, f32[4,80,1024]{2,1,0:T(8,128)S(1)} %pad_maximum_fusion.packed_ref), custom_call_target="tpu_custom_call" | custom-call | flops 17179869184 | bytes 4194304 | tf_op jit(solution)/shard_map/own_pairs/pallas_call | solution.py:171
  29.5 1.8 %collective-permute-done.2.prior_ref = f32[4,80,1024]{2,1,0:T(8,128)S(1)} collective-permute-done((f32[4,80,1024]{2,1,0:T(8,128)S(1)}, f32[4,80,1024]{2,1,0:T(8,128)S(1)}, u32[]{:S(2)}, u32[]{:S(2)}) %collective-permute-start.2) | collective-permute-done | bytes 1310752 | tf_op jit(solution)/shard_map/ppermute | solution.py:301
  31.4 2.5 %collective-permute-done.3.next_ref = f32[4,80,1024]{2,1,0:T(8,128)S(1)} collective-permute-done((f32[4,80,1024]{2,1,0:T(8,128)S(1)}, f32[4,80,1024]{2,1,0:T(8,128)S(1)}, u32[]{:S(2)}, u32[]{:S(2)}) %collective-permute-start.3) | collective-permute-done | bytes 1310752 | tf_op jit(solution)/shard_map/ppermute | solution.py:302
  33.8 41.4 %blk_pairs.1.before_ref = f32[4,16,1024]{2,1,0:T(8,128)S(1)} custom-call(s32[4,8]{1,0:T(4,128)S(1)} %bitcast.9, f32[4,80,1024]{2,1,0:T(8,128)S(1)} %collective-permute-done.2.prior_ref, f32[4,80,1024]{2,1,0:T(8,128)S(1)} %collective-permute-done.3.next_ref, bf16[4,256,1024]{2,1,0:T(8,128)(2,1)S(1)} %get-tuple-element.5.row_ref, ...), custom_call_target="tpu_custom_call" | custom-call | flops 25769803776 | bytes 4194304 | tf_op jit(solution)/shard_map/blk_pairs/pallas_call | solution.py:189
  75.3 0.0 copy-start.3
  75.3 0.0 copy-start.4
  75.3 0.0 copy-start.5
  75.3 0.0 collective-permute-done.prior_ref
  75.3 0.0 collective-permute-done.1.next_ref
  75.3 15.5 %grp_pairs.1.part_ref = f32[4,16,1024]{2,1,0:T(8,128)S(1)} custom-call(s32[4,8]{1,0:T(4,128)S(1)} %bitcast.10, f32[4,80,1024]{2,1,0:T(8,128)S(1)} %collective-permute-done.prior_ref, f32[4,80,1024]{2,1,0:T(8,128)S(1)} %collective-permute-done.1.next_ref, bf16[4,256,1024]{2,1,0:T(8,128)(2,1)S(1)} %get-tuple-element.5.row_ref, ...), custom_call_target="tpu_custom_call" | custom-call | flops 25769803776 | bytes 4194304 | tf_op jit(solution)/shard_map/grp_pairs/pallas_call | solution.py:189
  90.8 0.0 copy-start
  90.8 0.7 copy-done
  91.5 25.9 %sums.1 = f32[16,128]{1,0:T(8,128)} custom-call(f32[4,16,1024]{2,1,0:T(8,128)} %copy-done, f32[4,16,1024]{2,1,0:T(8,128)} %bitcast.13, f32[4,16,1024]{2,1,0:T(8,128)} %bitcast.11), custom_call_target="tpu_custom_call" | custom-call | tf_op jit(solution)/shard_map/sums/pallas_call | solution.py:276
  117.4 1.0 slice_reduce_fusion
  118.4 0.0 copy-done.4
  118.4 2.0 %multiply_add_fusion = (f32[1,1,4,16,1024]{4,3,2,1,0:T(8,128)}, f32[1,1,4,16,1024]{4,3,2,1,0:T(8,128)}, f32[1,1,4,16,1024]{4,3,2,1,0:T(8,128)}) fusion(f32[1,1,4,16,1024]{4,3,2,1,0:T(8,128)S(1)} %copy-done.3, f32[16]{0:T(128)S(1)} %get-tuple-element.7, f32[1,1,4,16,1024]{4,3,2,1,0:T(8,128)S(1)} %copy-done.4, f32[4,16,1024]{2,1,0:T(8,128)} %copy-done, ...), kind=kLoop, calls=%fused_computation.3 | loop fusion | flops 393216 | bytes 1835136 | tf_op jit(solution)/shard_map/add | solution.py:312
  (4 shorter events, 0.0 us)
Async XLA Ops:
  0.6 1.5 %copy-start.2 = (f32[1,1,4,16,1024]{4,3,2,1,0:T(8,128)S(1)}, f32[1,1,4,16,1024]{4,3,2,1,0:T(8,128)}, u32[]{:S(2)}) copy-start(f32[1,1,4,16,1024]{4,3,2,1,0:T(8,128)} %param.10) | copy-start | bytes 786436
  2.1 8.2 %copy-start.1 = (s32[1,1,4,8]{3,2,1,0:T(4,128)S(1)}, s32[1,1,4,8]{3,2,1,0:T(4,128)}, u32[]{:S(2)}) copy-start(s32[1,1,4,8]{3,2,1,0:T(4,128)} %param.11) | copy-start | bytes 388
  2.3 29.1 %collective-permute-start.2 = (f32[4,80,1024]{2,1,0:T(8,128)S(1)}, f32[4,80,1024]{2,1,0:T(8,128)S(1)}, u32[]{:S(2)}, u32[]{:S(2)}) collective-permute-start(f32[4,80,1024]{2,1,0:T(8,128)S(1)} %pad_maximum_fusion.packed_ref), channel_id=1, source_target_pairs={{0,8},{8,16},{16,24},{24,0},{1,9},{9,17},{17,25},{25,1},{2,10},{10... | collective-permute-start | bytes 3932168 | tf_op jit(solution)/shard_map/ppermute | solution.py:301
  2.8 31.1 %collective-permute-start.3 = (f32[4,80,1024]{2,1,0:T(8,128)S(1)}, f32[4,80,1024]{2,1,0:T(8,128)S(1)}, u32[]{:S(2)}, u32[]{:S(2)}) collective-permute-start(f32[4,80,1024]{2,1,0:T(8,128)S(1)} %pad_maximum_fusion.packed_ref), channel_id=1, source_target_pairs={{8,0},{16,8},{24,16},{0,24},{9,1},{17,9},{25,17},{1,25},{10,2},{18... | collective-permute-start | bytes 3932168 | tf_op jit(solution)/shard_map/ppermute | solution.py:302
  4.7 70.6 %collective-permute-start = (f32[4,80,1024]{2,1,0:T(8,128)S(1)}, f32[4,80,1024]{2,1,0:T(8,128)S(1)}, u32[]{:S(2)}, u32[]{:S(2)}) collective-permute-start(f32[4,80,1024]{2,1,0:T(8,128)S(1)} %pad_maximum_fusion.packed_ref), channel_id=1, source_target_pairs={{0,1},{1,2},{2,3},{3,4},{4,5},{5,6},{6,7},{8,9},{9,10},{10,11},{11... | collective-permute-start | bytes 3932168 | tf_op jit(solution)/shard_map/ppermute | solution.py:303
  9.0 66.3 %collective-permute-start.1 = (f32[4,80,1024]{2,1,0:T(8,128)S(1)}, f32[4,80,1024]{2,1,0:T(8,128)S(1)}, u32[]{:S(2)}, u32[]{:S(2)}) collective-permute-start(f32[4,80,1024]{2,1,0:T(8,128)S(1)} %pad_maximum_fusion.packed_ref), channel_id=1, source_target_pairs={{1,0},{2,1},{3,2},{4,3},{5,4},{6,5},{7,6},{9,8},{10,9},{11,10},{12... | collective-permute-start | bytes 3932168 | tf_op jit(solution)/shard_map/ppermute | solution.py:304
  75.3 43.1 %copy-start.3 = (f32[1,1,4,16,1024]{4,3,2,1,0:T(8,128)S(1)}, f32[1,1,4,16,1024]{4,3,2,1,0:T(8,128)}, u32[]{:S(2)}) copy-start(f32[1,1,4,16,1024]{4,3,2,1,0:T(8,128)} %param.10) | copy-start | bytes 786436
  75.3 43.1 %copy-start.4 = (f32[1,1,4,16,1024]{4,3,2,1,0:T(8,128)S(1)}, f32[1,1,4,16,1024]{4,3,2,1,0:T(8,128)}, u32[]{:S(2)}) copy-start(f32[1,1,4,16,1024]{4,3,2,1,0:T(8,128)} %param.9) | copy-start | bytes 786436
  75.3 43.1 %copy-start.5 = (f32[1,1,4,16,1024]{4,3,2,1,0:T(8,128)S(1)}, f32[1,1,4,16,1024]{4,3,2,1,0:T(8,128)}, u32[]{:S(2)}) copy-start(f32[1,1,4,16,1024]{4,3,2,1,0:T(8,128)} %param.8) | copy-start | bytes 786436
  90.8 0.7 copy-start

commit v3 on v2

--- a/solution.py
+++ b/solution.py
@@ -10,7 +10,7 @@
 NOISE = 0.5
 ROWS = 512
 COLS = 256
-LIMIT = 48 * 1024 * 1024
+LIMIT = 24 * 1024 * 1024
 MESH = pl.DeviceIdType.MESH
 
 
@@ -125,24 +125,62 @@
         part_ref[k] = NOISE * packed_ref[k, feat:] + folded(acc_ref, k, nvec)
 
 
-def side_kernel(feat, along_blk, ids_ref, prior_ref, next_ref, row_ref, before_ref, part_ref, col_ref, vec_ref, acc_ref):
+def build_columns(sources, feat, col_ref, vec_ref):
+    for k, (ref, tile) in enumerate(sources):
+        col_ref[k] = operand_rows(ref[tile, :feat], False).astype(jnp.bfloat16).T
+        vec_ref[k] = vector_rows(ref[tile, feat:])
+
+
+def near_step():
+    return 1 - 2 * lax.rem(lax.axis_index("grp"), 2)
+
+
+def mid_kernel(feat, ids_ref, prior_ref, next_ref, near_ref, row_ref, before_ref, part_ref, col_ref, vec_ref, acc_ref):
     tiles = prior_ref.shape[0]
     nvec = prior_ref.shape[1] - feat
-    for source, ref in enumerate((prior_ref, next_ref)):
-        for k in range(tiles):
-            col_ref[source * tiles + k] = operand_rows(ref[k, :feat], False).astype(jnp.bfloat16).T
-            vec_ref[source * tiles + k] = vector_rows(ref[k, feat:])
+    build_columns([(ref, k) for ref in (prior_ref, next_ref, near_ref) for k in range(tiles)], feat, col_ref, vec_ref)
     acc_ref[...] = jnp.zeros_like(acc_ref)
 
     def slot_of(step_blk, step_grp, within):
-        if along_blk:
-            return jnp.where(step_blk == 0, -1, jnp.where(step_blk == 1, tiles + within, within))
-        side = jnp.where(step_grp < 0, within, tiles + within)
-        return jnp.where((step_blk == 0) & (step_grp != 0), side, -1)
+        beside = jnp.where(step_grp == near_step(), 2 * tiles + within, -1)
+        return jnp.where(step_blk == 0, beside, jnp.where(step_blk == 1, tiles + within, within))
 
     walk(ids_ref, slot_of, row_ref, col_ref, vec_ref, acc_ref)
     for k in range(tiles):
         part_ref[k] = before_ref[k] + folded(acc_ref, k, nvec)
+
+
+def far_kernel(
+    feat, ids_ref, far_ref, row_ref, before_ref, residual_ref, direction_ref, part_ref, sums_ref, col_ref, vec_ref, acc_ref
+):
+    tiles = far_ref.shape[0]
+    nvec = far_ref.shape[1] - feat
+    build_columns([(far_ref, k) for k in range(tiles)], feat, col_ref, vec_ref)
+    acc_ref[...] = jnp.zeros_like(acc_ref)
+
+    def slot_of(step_blk, step_grp, within):
+        return jnp.where((step_blk == 0) & (step_grp == -near_step()), within, -1)
+
+    walk(ids_ref, slot_of, row_ref, col_ref, vec_ref, acc_ref)
+    for k in range(tiles):
+        part_ref[k] = before_ref[k] + folded(acc_ref, k, nvec)
+    lane = lax.broadcasted_iota(jnp.int32, (nvec, 128), 1)
+    part, residual, direction = part_ref[...], residual_ref[...], direction_ref[...]
+    held = jnp.zeros((nvec, 128), jnp.float32)
+    for k, both in enumerate((residual * residual, direction * part, residual * part, part * part)):
+        total = jnp.sum(jnp.sum(both, axis=0), axis=1, keepdims=True)
+        held = jnp.where(lane == k, total, held)
+    sums_ref[...] = held
+
+
+def update_kernel(factors_ref, part_ref, solution_ref, residual_ref, direction_ref, x_ref, r_ref, d_ref):
+    step, ratio = factors_ref[:, :1], factors_ref[:, 1:2]
+    for k in range(part_ref.shape[0]):
+        direction = direction_ref[k]
+        residual = residual_ref[k] - step * part_ref[k]
+        x_ref[k] = solution_ref[k] + step * direction
+        r_ref[k] = residual
+        d_ref[k] = residual + ratio * direction
 
 
 def scratch(cols, feat, nvec, tiles, tile):
@@ -183,22 +221,52 @@
     )(ids, packed)
 
 
-def side_pairs(ids, prior, following, rows, before, feat, along_blk):
+def mid_pairs(ids, prior, following, near, rows, before, feat):
     tiles, width, tile = prior.shape
     nvec = width - feat
     return pl.pallas_call(
-        functools.partial(side_kernel, feat, along_blk),
+        functools.partial(mid_kernel, feat),
         out_shape=jax.ShapeDtypeStruct((tiles, nvec, tile), jnp.float32),
-        in_specs=[in_smem()] + [in_vmem()] * 4,
+        in_specs=[in_smem()] + [in_vmem()] * 5,
         out_specs=in_vmem(),
-        scratch_shapes=scratch(2 * tiles, feat, nvec, tiles, tile),
+        scratch_shapes=scratch(3 * tiles, feat, nvec, tiles, tile),
         compiler_params=pltpu.CompilerParams(vmem_limit_bytes=LIMIT),
-        cost_estimate=cost(12, tile),
-        name="blk_pairs" if along_blk else "grp_pairs",
-    )(ids, prior, following, rows, before)
-
-
-def sums_kernel(part_ref, residual_ref, direction_ref, out_ref, held_ref, blk_ref, grp_ref, send_sem, blk_sem, grp_sem):
+        cost_estimate=cost(18, tile),
+        name="mid_pairs",
+    )(ids, prior, following, near, rows, before)
+
+
+def far_pairs(ids, far, rows, before, residual, direction, feat):
+    tiles, width, tile = far.shape
+    nvec = width - feat
+    return pl.pallas_call(
+        functools.partial(far_kernel, feat),
+        out_shape=(
+            jax.ShapeDtypeStruct((tiles, nvec, tile), jnp.float32),
+            jax.ShapeDtypeStruct((nvec, 128), jnp.float32),
+        ),
+        in_specs=[in_smem()] + [in_vmem()] * 5,
+        out_specs=(in_vmem(), in_vmem()),
+        scratch_shapes=scratch(tiles, feat, nvec, tiles, tile),
+        compiler_params=pltpu.CompilerParams(vmem_limit_bytes=LIMIT),
+        cost_estimate=cost(6, tile),
+        name="far_pairs",
+    )(ids, far, rows, before, residual, direction)
+
+
+def updated(factors, part, *state):
+    shape = jax.ShapeDtypeStruct(part.shape, jnp.float32)
+    return pl.pallas_call(
+        update_kernel,
+        out_shape=(shape, shape, shape),
+        in_specs=[in_vmem()] * 5,
+        out_specs=(in_vmem(), in_vmem(), in_vmem()),
+        compiler_params=pltpu.CompilerParams(vmem_limit_bytes=LIMIT),
+        name="updated",
+    )(factors, part, *state)
+
+
+def sums_kernel(sums_ref, out_ref, held_ref, blk_ref, grp_ref, send_sem, blk_sem, grp_sem):
     blk_count, grp_count = lax.axis_size("blk"), lax.axis_size("grp")
     blk_index, grp_index = lax.axis_index("blk"), lax.axis_index("grp")
     barrier = pltpu.get_barrier_semaphore()
@@ -216,23 +284,7 @@
     lax.fori_loop(1, blk_count, functools.partial(greet, blk_partner), 0)
     lax.fori_loop(1, grp_count, functools.partial(greet, grp_partner), 0)
 
-    nvec = part_ref.shape[1]
-    lane = lax.broadcasted_iota(jnp.int32, (nvec, 128), 1)
-
-    def total_of(first_ref, second_ref):
-        both = jnp.sum(first_ref[...] * second_ref[...], axis=0)
-        return jnp.sum(both, axis=1, keepdims=True)
-
-    held = jnp.zeros((nvec, 128), jnp.float32)
-    pairs = (
-        (residual_ref, residual_ref),
-        (direction_ref, part_ref),
-        (residual_ref, part_ref),
-        (part_ref, part_ref),
-    )
-    for k, (first_ref, second_ref) in enumerate(pairs):
-        held = jnp.where(lane == k, total_of(first_ref, second_ref), held)
-    held_ref[0] = held
+    held_ref[0] = sums_ref[...]
     pl.semaphore_wait(barrier, blk_count + grp_count - 2)
 
     def swap(source, landing, sems, partner, count):
@@ -267,16 +319,17 @@
     start_norm, curvature, crossed, length = (sums[:, k : k + 1] for k in range(4))
     step = start_norm / curvature
     fresh_norm = jnp.maximum(start_norm + step * (step * length - 2.0 * crossed), 0.0)
+    lane = lax.broadcasted_iota(jnp.int32, sums.shape, 1)
     out_ref[...] = jnp.where(lane == 0, step, fresh_norm / start_norm)
 
 
-def summed(part, residual, direction):
-    nvec = part.shape[1]
+def summed(sums):
+    nvec = sums.shape[0]
     blk_count, grp_count = lax.axis_size("blk"), lax.axis_size("grp")
     return pl.pallas_call(
         sums_kernel,
         out_shape=jax.ShapeDtypeStruct((nvec, 128), jnp.float32),
-        in_specs=[in_vmem()] * 3,
+        in_specs=[in_vmem()],
         out_specs=in_vmem(),
         scratch_shapes=[
             pltpu.VMEM((2, nvec, 128), jnp.float32),
@@ -288,7 +341,7 @@
         ],
         compiler_params=pltpu.CompilerParams(collective_id=0, has_side_effects=True),
         name="sums",
-    )(part, residual, direction)
+    )(sums)
 
 
 def per_device(features, inv_scale, solution, residual, direction, neighbours):
@@ -298,19 +351,19 @@
     ids = neighbours[0, 0]
     up = [(i, (i + 1) % blk_count) for i in range(blk_count)]
     down = [((i + 1) % blk_count, i) for i in range(blk_count)]
+    swapped = [(i, i + 1 - 2 * (i % 2)) for i in range(grp_count)]
+    handed = [(i, i + 2) for i in range(0, grp_count - 2, 2)] + [(i, i - 2) for i in range(3, grp_count, 2)]
+    near = lax.ppermute(packed, "grp", swapped)
     prior_blk = lax.ppermute(packed, "blk", up)
     next_blk = lax.ppermute(packed, "blk", down)
-    prior_grp = lax.ppermute(packed, "grp", [(i, i + 1) for i in range(grp_count - 1)])
-    next_grp = lax.ppermute(packed, "grp", [(i + 1, i) for i in range(grp_count - 1)])
     rows, part = own_pairs(ids, packed, feat)
-    part = side_pairs(ids, prior_blk, next_blk, rows, part, feat, True)
-    part = side_pairs(ids, prior_grp, next_grp, rows, part, feat, False)
-    factors = summed(part, residual[0, 0], direction[0, 0])
-    step, ratio = factors[:, :1], factors[:, 1:2]
-    new_residual = residual - step * part
-    new_solution = solution + step * direction
-    new_direction = new_residual + ratio * direction
-    return (new_solution, new_residual, new_direction)
+    near, part = lax.optimization_barrier((near, part))
+    far = lax.ppermute(near, "grp", handed)
+    part = mid_pairs(ids, prior_blk, next_blk, near, rows, part, feat)
+    part, sums = far_pairs(ids, far, rows, part, residual[0, 0], direction[0, 0], feat)
+    factors = summed(sums)
+    outs = updated(factors, part, solution[0, 0], residual[0, 0], direction[0, 0])
+    return tuple(out[None, None] for out in outs)
 
 
 def solution(mesh):

time: 120 us -> 115 us (0.958)
  Pallas kernels: 102 us -> 100 us
  other arithmetic: 3.55 us -> 1.6 us
    pallas_call x1, Pallas kernels: 19.2 us -> 25.2 us  [own_pairs(): pl.pallas_call(functools.partial(own_kernel, feat), out_shape=(jax.ShapeD...]
    pallas_call x2 -> x3, Pallas kernels: 56.9 us -> 51.4 us  [the longest x1 48 us: mid_pairs(): pl.pallas_call(functools.partial(mid_kernel, feat), out_shape=jax.ShapeDt...]
    ppermute x2, waiting for transfers between devices: 0.01 us -> 4.65 us  [the longest x1 4.64 us: per_device(): near = lax.ppermute(packed, 'grp', swapped)]
    pallas_call x1, Pallas kernels: 25.9 us -> 23.4 us  [summed(): pl.pallas_call(sums_kernel, out_shape=jax.ShapeDtypeStruct((nvec, 128), j...]
    ppermute x1, waiting for transfers between devices: 2.49 us -> 0.01 us  [per_device(): next_blk = lax.ppermute(packed, 'blk', down)]
    add x1 -> x0, other arithmetic: 1.97 us -> none  [per_device(): new_direction = new_residual + ratio * direction]
    ppermute x1, waiting for transfers between devices: 1.84 us -> 0.01 us  [per_device(): prior_blk = lax.ppermute(packed, 'blk', up)]
  transfers between devices with their start and end apart: 4 -> 4, of which waited for: 2 -> 1; matrix products, arithmetic and copies ran while one was open for 0% -> 0% of each run, Pallas kernels for 50% -> 63%
where the time goes in v3:
time: 115 us; the launch traced here: 116 us
  Pallas kernels  100 us (87%)
  starting transfers between devices  7.5 us (7%)
  waiting for transfers between devices  4.65 us (4%)
  other arithmetic  1.6 us (1%)
  local copies, waits for them, and re-layouts  1.32 us (1%)
    pallas_call x1, Pallas kernels, mid_pairs(): pl.pallas_call(functools.partial(mid_kernel, feat), out_shape=jax.ShapeDt...  48 us
    pallas_call x1, Pallas kernels, own_pairs(): pl.pallas_call(functools.partial(own_kernel, feat), out_shape=(jax.ShapeD...  25.2 us
    pallas_call x1, Pallas kernels, summed(): pl.pallas_call(sums_kernel, out_shape=jax.ShapeDtypeStruct((nvec, 128), j...  23.4 us
    ppermute x1, waiting for transfers between devices, per_device(): near = lax.ppermute(packed, 'grp', swapped)  4.64 us
    ppermute x1, starting transfers between devices, per_device(): far = lax.ppermute(near, 'grp', handed)  3.55 us
    ppermute x1, starting transfers between devices, per_device(): next_blk = lax.ppermute(packed, 'blk', down)  2.43 us
    pallas_call x1, Pallas kernels, far_pairs(): pl.pallas_call(functools.partial(far_kernel, feat), out_shape=(jax.ShapeD...  2.42 us
  transfers between devices with their start and end apart: 4, of which 1 were waited for; matrix products, arithmetic and copies ran while one was open for 0% of the time, Pallas kernels for 63%

profile of v3, /device:TPU:0, one launch (start us, length us, event | category | flops | bytes accessed | tf_op | source)
XLA Modules:
  0.0 115.9 jit_solution(1068196353657809466)
XLA Ops:
  0.6 0.0 copy-start
  0.6 1.5 %bitcast_multiply_fusion = f32[4,64,1024]{2,1,0:T(8,128)S(1)} fusion(f32[1,1,4,64,1024]{4,3,2,1,0:T(8,128)} %param.6, f32[64]{0:T(128)} %param.7), kind=kLoop, calls=%fused_computation.1 | loop fusion | flops 262144 | bytes 2097408 | tf_op jit(solution)/shard_map/mul | solution.py:350
  2.1 0.0 copy-done
  2.1 0.0 copy-start.5
  2.1 0.1 pad_maximum_fusion.packed_ref
  2.3 2.4 %collective-permute-start.3 = (f32[4,80,1024]{2,1,0:T(8,128)S(1)}, f32[4,80,1024]{2,1,0:T(8,128)S(1)}, u32[]{:S(2)}, u32[]{:S(2)}) collective-permute-start(f32[4,80,1024]{2,1,0:T(8,128)S(1)} %pad_maximum_fusion.packed_ref), channel_id=1, source_target_pairs={{8,0},{16,8},{24,16},{0,24},{9,1},{17,9},{25,17},{1,25},{10,2},{18... | collective-permute-start | bytes 3932168 | tf_op jit(solution)/shard_map/ppermute | solution.py:358
  4.7 0.0 collective-permute-start.2
  4.7 1.5 %collective-permute-start = (f32[4,80,1024]{2,1,0:T(8,128)S(1)}, f32[4,80,1024]{2,1,0:T(8,128)S(1)}, u32[]{:S(2)}, u32[]{:S(2)}) collective-permute-start(f32[4,80,1024]{2,1,0:T(8,128)S(1)} %pad_maximum_fusion.packed_ref), channel_id=1, source_target_pairs={{0,1},{1,0},{2,3},{3,2},{4,5},{5,4},{6,7},{7,6},{8,9},{9,8},{10,11... | collective-permute-start | bytes 3932168 | tf_op jit(solution)/shard_map/ppermute | solution.py:356
  6.2 0.0 copy-done.5
  6.2 25.2 %own_pairs.1 = (bf16[4,256,1024]{2,1,0:T(8,128)(2,1)S(1)}, f32[4,16,1024]{2,1,0:T(8,128)S(1)}) custom-call(s32[4,8]{1,0:T(4,128)S(1)} %bitcast.15, f32[4,80,1024]{2,1,0:T(8,128)S(1)} %pad_maximum_fusion.packed_ref), custom_call_target="tpu_custom_call" | custom-call | flops 17179869184 | bytes 4194304 | tf_op jit(solution)/shard_map/own_pairs/pallas_call | solution.py:209
  31.5 4.6 %collective-permute-done.near_ref = f32[4,80,1024]{2,1,0:T(8,128)S(1)} collective-permute-done((f32[4,80,1024]{2,1,0:T(8,128)S(1)}, f32[4,80,1024]{2,1,0:T(8,128)S(1)}, u32[]{:S(2)}, u32[]{:S(2)}) %collective-permute-start) | collective-permute-done | bytes 1310752 | tf_op jit(solution)/shard_map/ppermute | solution.py:356
  36.1 3.6 %collective-permute-start.1 = (f32[4,80,1024]{2,1,0:T(8,128)S(1)}, f32[4,80,1024]{2,1,0:T(8,128)S(1)}, u32[]{:S(2)}, u32[]{:S(2)}) collective-permute-start(f32[4,80,1024]{2,1,0:T(8,128)S(1)} %collective-permute-done.near_ref), channel_id=1, source_target_pairs={{0,2},{2,4},{4,6},{3,1},{5,3},{7,5},{8,10},{10,12},{12,14},{11,9},... | collective-permute-start | bytes 3932168 | tf_op jit(solution)/shard_map/ppermute | solution.py:361
  39.7 0.0 collective-permute-done.3.next_ref
  39.7 0.0 collective-permute-done.2.prior_ref
  39.7 0.0 copy-start.1
  39.7 48.0 %mid_pairs.1.before_ref = f32[4,16,1024]{2,1,0:T(8,128)S(1)} custom-call(s32[4,8]{1,0:T(4,128)S(1)} %bitcast.16, f32[4,80,1024]{2,1,0:T(8,128)S(1)} %collective-permute-done.2.prior_ref, f32[4,80,1024]{2,1,0:T(8,128)S(1)} %collective-permute-done.3.next_ref, f32[4,80,1024]{2,1,0:T(8,128)S(1)} %collective-permute-done.near_ref, ...), custom_call_target="tpu_custom_call" | custom-call | flops 38654705664 | bytes 4194304 | tf_op jit(solution)/shard_map/mid_pairs/pallas_call | solution.py:227
  87.7 0.0 collective-permute-done.1.far_ref
  87.7 0.0 copy-done.1
  87.7 0.0 copy-start.2
  87.7 2.4 %far_pairs.1 = (f32[4,16,1024]{2,1,0:T(8,128)S(1)}, f32[16,128]{1,0:T(8,128)S(1)}) custom-call(s32[4,8]{1,0:T(4,128)S(1)} %bitcast.17, f32[4,80,1024]{2,1,0:T(8,128)S(1)} %collective-permute-done.1.far_ref, bf16[4,256,1024]{2,1,0:T(8,128)(2,1)S(1)} %get-tuple-element.14.row_ref, f32[4,16,1024]{2,1,0:T(8,128)S(1)} %mid_pairs.1.before_ref, ...), custom_call_target="tpu_custom_call" | custom-call | flops 12884901888 | bytes 4194304 | tf_op jit(solution)/shard_map/far_pairs/pallas_call | solution.py:242
  90.2 0.6 copy-done.4
  90.8 23.4 %sums.1.factors_ref = f32[16,128]{1,0:T(8,128)} custom-call(f32[16,128]{1,0:T(8,128)} %copy-done.4), custom_call_target="tpu_custom_call" | custom-call | tf_op jit(solution)/shard_map/sums/pallas_call | solution.py:329
  114.2 0.7 copy-done.3
  114.9 1.0 updated.1
  (3 shorter events, 0.0 us)
Async XLA Ops:
  0.6 1.5 %copy-start = (f32[1,1,4,16,1024]{4,3,2,1,0:T(8,128)S(1)}, f32[1,1,4,16,1024]{4,3,2,1,0:T(8,128)}, u32[]{:S(2)}) copy-start(f32[1,1,4,16,1024]{4,3,2,1,0:T(8,128)} %param.10) | copy-start | bytes 786436
  2.1 4.1 %copy-start.5 = (s32[1,1,4,8]{3,2,1,0:T(4,128)S(1)}, s32[1,1,4,8]{3,2,1,0:T(4,128)}, u32[]{:S(2)}) copy-start(s32[1,1,4,8]{3,2,1,0:T(4,128)} %param.11) | copy-start | bytes 388
  2.3 37.4 %collective-permute-start.3 = (f32[4,80,1024]{2,1,0:T(8,128)S(1)}, f32[4,80,1024]{2,1,0:T(8,128)S(1)}, u32[]{:S(2)}, u32[]{:S(2)}) collective-permute-start(f32[4,80,1024]{2,1,0:T(8,128)S(1)} %pad_maximum_fusion.packed_ref), channel_id=1, source_target_pairs={{8,0},{16,8},{24,16},{0,24},{9,1},{17,9},{25,17},{1,25},{10,2},{18... | collective-permute-start | bytes 3932168 | tf_op jit(solution)/shard_map/ppermute | solution.py:358
  4.7 35.0 %collective-permute-start.2 = (f32[4,80,1024]{2,1,0:T(8,128)S(1)}, f32[4,80,1024]{2,1,0:T(8,128)S(1)}, u32[]{:S(2)}, u32[]{:S(2)}) collective-permute-start(f32[4,80,1024]{2,1,0:T(8,128)S(1)} %pad_maximum_fusion.packed_ref), channel_id=1, source_target_pairs={{0,8},{8,16},{16,24},{24,0},{1,9},{9,17},{17,25},{25,1},{2,10},{10... | collective-permute-start | bytes 3932168 | tf_op jit(solution)/shard_map/ppermute | solution.py:357
  4.7 31.4 %collective-permute-start = (f32[4,80,1024]{2,1,0:T(8,128)S(1)}, f32[4,80,1024]{2,1,0:T(8,128)S(1)}, u32[]{:S(2)}, u32[]{:S(2)}) collective-permute-start(f32[4,80,1024]{2,1,0:T(8,128)S(1)} %pad_maximum_fusion.packed_ref), channel_id=1, source_target_pairs={{0,1},{1,0},{2,3},{3,2},{4,5},{5,4},{6,7},{7,6},{8,9},{9,8},{10,11... | collective-permute-start | bytes 3932168 | tf_op jit(solution)/shard_map/ppermute | solution.py:356
  36.1 51.6 %collective-permute-start.1 = (f32[4,80,1024]{2,1,0:T(8,128)S(1)}, f32[4,80,1024]{2,1,0:T(8,128)S(1)}, u32[]{:S(2)}, u32[]{:S(2)}) collective-permute-start(f32[4,80,1024]{2,1,0:T(8,128)S(1)} %collective-permute-done.near_ref), channel_id=1, source_target_pairs={{0,2},{2,4},{4,6},{3,1},{5,3},{7,5},{8,10},{10,12},{12,14},{11,9},... | collective-permute-start | bytes 3932168 | tf_op jit(solution)/shard_map/ppermute | solution.py:361
  39.7 48.0 %copy-start.1 = (f32[1,1,4,16,1024]{4,3,2,1,0:T(8,128)S(1)}, f32[1,1,4,16,1024]{4,3,2,1,0:T(8,128)}, u32[]{:S(2)}) copy-start(f32[1,1,4,16,1024]{4,3,2,1,0:T(8,128)} %param.9) | copy-start | bytes 786436
  87.7 26.4 %copy-start.2 = (f32[1,1,4,16,1024]{4,3,2,1,0:T(8,128)S(1)}, f32[1,1,4,16,1024]{4,3,2,1,0:T(8,128)}, u32[]{:S(2)}) copy-start(f32[1,1,4,16,1024]{4,3,2,1,0:T(8,128)} %param.8) | copy-start | bytes 786436
  90.2 0.6 copy-start.4
  114.2 0.7 copy-start.3
